TPU v7x, 32 devices: a whole 2x2x4 slice. The times are simulated.
32 devices in a mesh: frame: 4 (over z), tile: 8 (over y, x, core).
Axes of the slice: x: 2, y: 2, z: 4, core: 2. Of those that a mesh axis runs over, the one named last changes fastest.
Arguments:
- displacement: bfloat16 [512, 2, 8, 4096], P('frame', None, 'tile'), may hold values from -256 to 256
Outputs:
- basis: bfloat16 [512, 3, 8, 4096], P(None, None, 'tile', 'frame')
- factor: float32 [512, 512], replicated
All inputs are finite; a program needn't handle non-finite values.
Results may differ from a plain program's by a relative error of at most 0.0053.
The roundings to bfloat16 on the way count: a program that leaves them out, or rounds other values in their place, can miss the bound.
Values may be sent and summed in bfloat16 or wider, within the bound.
A program may use at most 64 MiB of HBM per device.

v0:
```python
import math

import jax
import jax.numpy as jnp
from jax import lax
from jax.sharding import PartitionSpec as P


def with_halo(array, sides, width):
    for axis, dim in sides:
        peers, length = (lax.axis_size(axis), array.shape[dim])
        up = [(i, (i + 1) % peers) for i in range(peers - 1)]
        down = [(j, i) for i, j in up]
        last = lax.slice_in_dim(array, length - width, length, axis=dim)
        first = lax.slice_in_dim(array, 0, width, axis=dim)
        before = lax.ppermute(last, axis, up)
        after = lax.ppermute(first, axis, down)
        array = jnp.concatenate([before, array, after], axis=dim)
    return array


def derivative(center, before, after, first, final):
    return jnp.where(
        first, after - center, jnp.where(final, center - before, (after - before) * 0.5)
    )


def column_derivative(center):
    width = center.shape[-1]
    after = jnp.concatenate([center[..., 1:], center[..., -1:]], axis=-1)
    before = jnp.concatenate([center[..., :1], center[..., :-1]], axis=-1)
    column = jnp.arange(width, dtype=jnp.int32)
    return derivative(center, before, after, column == 0, column == width - 1)


def combine_strain(d_rows, d_cols):
    return jnp.stack(
        [d_cols[:, 0], d_rows[:, 1], 0.5 * (d_rows[:, 0] + d_cols[:, 1])], axis=1
    ).astype(jnp.bfloat16)


def local(displacement):
    rows = displacement.shape[2]
    full_width = displacement.shape[3]
    total_rows = lax.axis_size("tile") * rows
    scale = math.sqrt(3 * total_rows * full_width)
    row_global = lax.axis_index("tile") * rows + jnp.arange(rows, dtype=jnp.int32)
    first = (row_global == 0)[:, None]
    final = (row_global == total_rows - 1)[:, None]
    padded = with_halo(displacement, (("tile", 2),), 1)
    field = padded.astype(jnp.float32)
    center = field[:, :, 1:-1, :]
    d_rows = derivative(center, field[:, :, :-2, :], field[:, :, 2:, :], first, final)
    d_cols = column_derivative(center)
    strain = combine_strain(d_rows, d_cols)
    pixel_major = lax.all_to_all(strain, "frame", split_axis=3, concat_axis=0, tiled=True)
    frames = pixel_major.shape[0]
    snapshot_half = pixel_major.reshape(frames, -1)
    local_gram = lax.dot_general(
        snapshot_half, snapshot_half, (((1,), (1,)), ((), ())), preferred_element_type=jnp.float32
    )
    gram = lax.psum(local_gram, ("frame", "tile"))
    lower = jnp.linalg.cholesky(gram)
    snapshot = snapshot_half.astype(jnp.float32)
    solved = lax.linalg.triangular_solve(lower, snapshot, left_side=True, lower=True)
    basis = (solved * scale).astype(jnp.bfloat16).reshape(pixel_major.shape)
    return (basis, lower.T / scale)


def solution(mesh):
    return jax.shard_map(
        local,
        mesh=mesh,
        in_specs=(P("frame", None, "tile", None),),
        out_specs=(P(None, None, "tile", "frame"), P()),
        check_vma=False,
    )
```

profile of v0, /device:TPU:0, one launch (start us, length us, event | category | flops | bytes accessed | tf_op | source)
XLA Modules:
  0.0 550.1 jit_solution(10994254304683676860)
XLA Ops:
  7.2 8.5 %copy.30 = bf16[128,2,1,4096]{0,1,2,3:T(2,128)(2,1)S(1)} copy(bf16[128,2,1,4096]{3,1,2,0:T(2,128)(2,1)} %param.1) | data formatting | bytes 4194304 | tf_op args[0]
  15.7 3.7 collective-permute-start
  22.0 4.4 collective-permute-done.1
  26.3 9.6 %maximum_convert_fusion = f32[128,2,3,4096]{0,1,2,3:T(2,128)S(1)} fusion(bf16[128,2,1,4096]{0,1,2,3:T(2,128)(2,1)} %collective-permute-done.1, bf16[128,2,1,4096]{0,1,2,3:T(2,128)(2,1)S(1)} %copy.30, bf16[128,2,1,4096]{0,1,2,3:T(2,128)(2,1)} %collective-permute-done), kind=kLoop, calls=%fused_computation.2 | loop fusion | flops 9437184 | bytes 18874368 | tf_op jit(solution)/shard_map/convert_element_type | solution.py:51
  36.0 3.0 fusion.42
  39.0 22.9 %select_select_fusion = (f32[128,2,1,4096]{0,1,2,3:T(2,128)S(1)}, f32[128,2,1,4096]{0,1,2,3:T(2,128)S(1)}) fusion(f32[128,2,3,4096]{0,1,2,3:T(2,128)S(1)} %maximum_convert_fusion, pred[]{:T(512)S(6)} %eq.25, pred[]{:T(512)S(6)} %eq.24, f32[128,2,1,4095]{0,1,2,3:T(2,128)S(1)} %get-tuple-element.29, f32[128,2,1,1]{0,1,2,3:T(2,128)S(1)} %get-tuple-element.31, ...), kind=kLoop, calls=%fused_computation.14 | loop fusion | flops 14680064 | bytes 29368322 | tf_op jit(solution)/shard_map/jit(_where)/select_n | solution.py:23
  64.1 3.3 fusion.18
  68.9 7.1 %pad_maximum_fusion.2 = bf16[128,3,1,4096]{0,1,2,3:T(4,128)(2,1)S(1)} fusion(bf16[128,1,1,4096]{0,1,2,3:T(2,128)(2,1)S(1)} %fusion.18, bf16[128,1,1,4096]{0,1,2,3:T(2,128)(2,1)S(1)} %slice.188, bf16[128,1,1,4096]{0,1,2,3:T(2,128)(2,1)S(1)} %slice.189), kind=kLoop, calls=%fused_computation.13 | loop fusion | flops 9437184 | bytes 6291456 | tf_op jit(solution)/shard_map/stack | solution.py:37
  76.1 76.3 %all_to_all.15 = bf16[128,3,1,4096]{0,1,2,3:T(4,128)(2,1)S(1)} all-to-all(bf16[128,3,1,4096]{0,1,2,3:T(4,128)(2,1)S(1)} %pad_maximum_fusion.2), channel_id=1, replica_groups=mesh['frame'=4,'tile'=8] {'frame'}, dimensions={3} | all-to-all | bytes 6291456 | tf_op jit(solution)/shard_map/all_to_all | solution.py:56
  152.8 2.4 copy.34
  157.0 2.8 fusion.40
  163.3 3.3 copy.38
  166.6 5.4 convert_element_type.26
  171.9 178.4 %all-reduce.3.cloned.1.call-done = f32[512,512]{0,1:T(8,128)} async-done(((f32[512,512]{0,1:T(8,128)}), f32[512,512]{0,1:T(8,128)}) %all-reduce.3.cloned.1.call-update) | async-done | bytes 1048592 | tf_op jit(solution)/shard_map/psum | solution.py:62
  353.3 11.7 %cholesky.104 = f32[128,128]{1,0:T(8,128)S(1)} custom-call(f32[128,128]{1,0:T(8,128)S(1)} %cholesky.266), custom_call_target="Cholesky" | custom-call | tf_op jit(solution)/shard_map/jit(cholesky)/cholesky | solution.py:63
  365.2 9.8 %custom-call.30 = f32[1,128,128]{1,2,0:T(8,128)S(1)} custom-call(f32[1,128,128]{2,1,0:T(8,128)S(1)} %get-tuple-element.43), custom_call_target="InvertDiagBlocksLowerTriangular" | custom-call | tf_op jit(solution)/shard_map/jit(cholesky)/cholesky | solution.py:63
  375.7 11.7 %cholesky.217 = f32[128,128]{1,0:T(8,128)S(1)} custom-call(f32[128,128]{1,0:T(8,128)S(1)} %cholesky.270), custom_call_target="Cholesky" | custom-call | tf_op jit(solution)/shard_map/jit(cholesky)/cholesky | solution.py:63
  388.7 20.3 %custom-call.31 = f32[1,128,128]{1,2,0:T(8,128)S(1)} custom-call(f32[1,128,128]{2,1,0:T(8,128)S(1)} %get-tuple-element.40), custom_call_target="InvertDiagBlocksLowerTriangular" | custom-call | tf_op jit(solution)/shard_map/jit(cholesky)/cholesky | solution.py:63
  409.7 11.7 %cholesky.238 = f32[128,128]{1,0:T(8,128)S(1)} custom-call(f32[128,128]{1,0:T(8,128)S(1)} %cholesky.275), custom_call_target="Cholesky" | custom-call | tf_op jit(solution)/shard_map/jit(cholesky)/cholesky | solution.py:63
  422.1 9.8 %custom-call.32 = f32[1,128,128]{1,2,0:T(8,128)S(1)} custom-call(f32[1,128,128]{2,1,0:T(8,128)S(1)} %get-tuple-element.37), custom_call_target="InvertDiagBlocksLowerTriangular" | custom-call | tf_op jit(solution)/shard_map/jit(cholesky)/cholesky | solution.py:63
  432.5 11.7 %cholesky.255 = f32[128,128]{1,0:T(8,128)S(1)} custom-call(f32[128,128]{1,0:T(8,128)S(1)} %convolution_subtract_fusion.4), custom_call_target="Cholesky" | custom-call | tf_op jit(solution)/shard_map/jit(cholesky)/cholesky | solution.py:63
  448.8 10.4 %while.1 = (s32[]{:T(128)}, f32[512,512]{1,0:T(8,128)S(1)}, s32[4,2]{0,1:T(2,128)S(1)}, f32[4,128,128]{2,1,0:T(8,128)}, s32[]{:T(128)}) while((s32[]{:T(128)}, f32[512,512]{1,0:T(8,128)S(1)}, s32[4,2]{0,1:T(2,128)S(1)}, f32[4,128,128]{2,1,0:T(8,128)}, s32[]{:T(128)}) %tuple.38), condition=%wide.while_cond, body=%wide.while_body.sunk | while | flops 2 | bytes 132705 | solution.py:65
  459.2 41.0 %custom-call.33 = f32[4,128,128]{1,2,0:T(8,128)} custom-call(f32[4,128,128]{2,1,0:T(8,128)} %get-tuple-element.9), custom_call_target="InvertDiagBlocksLowerTriangular" | custom-call | tf_op jit(solution)/shard_map/triangular_solve | solution.py:65
  501.9 2.9 convolution_subtract_fusion
  506.4 3.4 convolution_subtract_fusion.1
  512.4 5.6 %fusion.10 = f32[3072,128]{0,1:T(8,128)} fusion(f32[128,3072]{1,0:T(8,128)S(1)} %fusion.29, f32[128,3072]{1,0:T(8,128)S(1)} %fusion.31, f32[128,3072]{1,0:T(8,128)S(1)} %fusion.32, f32[512,3072]{1,0:T(8,128)} %convert_element_type.26, f32[512,512]{1,0:T(8,128)} %copy-done.6), kind=kOutput, calls=%fused_computation.19 | convolution fusion | flops 1814691840 | bytes 8060928 | tf_op jit(solution)/shard_map/triangular_solve | solution.py:65
  517.9 3.0 copy.40
  524.2 3.2 copy.41
  527.4 2.9 convolution_bitcast_fusion
  532.0 3.2 copy.44
  536.7 2.6 copy.47
  539.4 3.5 fusion.13
  (70 shorter events, 43.7 us)
Async XLA Ops:
  7.2 343.1 %all-reduce.3.cloned.1.call-start = ((), (), s32[]{:S(2)}) async-start(), calls=%async_computation.1 | async-start | bytes 2097152 | tf_op jit(solution)/shard_map/psum | solution.py:62
  15.7 6.3 %collective-permute-start = (bf16[128,2,1,4096]{0,1,2,3:T(2,128)(2,1)S(1)}, bf16[128,2,1,4096]{0,1,2,3:T(2,128)(2,1)}, u32[]{:S(2)}, u32[]{:S(2)}) collective-permute-start(bf16[128,2,1,4096]{0,1,2,3:T(2,128)(2,1)S(1)} %copy.30), channel_id=1, source_target_pairs={{0,1},{1,2},{2,3},{3,4},{4,5},{5,6},{6,7},{8,9},{9,10},{10,11},{11... | collective-permute-start | bytes 6291464 | tf_op jit(solution)/shard_map/ppermute | solution.py:16
  19.3 7.0 %collective-permute-start.1 = (bf16[128,2,1,4096]{0,1,2,3:T(2,128)(2,1)S(1)}, bf16[128,2,1,4096]{0,1,2,3:T(2,128)(2,1)}, u32[]{:S(2)}, u32[]{:S(2)}) collective-permute-start(bf16[128,2,1,4096]{0,1,2,3:T(2,128)(2,1)S(1)} %copy.30), channel_id=1, source_target_pairs={{1,0},{2,1},{3,2},{4,3},{5,4},{6,5},{7,6},{9,8},{10,9},{11,10},{12... | collective-permute-start | bytes 6291464 | tf_op jit(solution)/shard_map/ppermute | solution.py:17
  155.3 1.7 copy-start.1
  375.7 124.5 %copy-start.5 = (bf16[1,128,3,1,1024]{1,4,0,2,3:T(8,128)(2,1)S(1)}, bf16[1,128,3,1,1024]{1,4,0,2,3:T(8,128)(2,1)}, u32[]{:S(2)}) copy-start(bf16[1,128,3,1,1024]{1,4,0,2,3:T(8,128)(2,1)} %triangular_solve.138) | copy-start | bytes 2359300
  459.2 42.7 %copy-start.6 = (f32[512,512]{1,0:T(8,128)}, f32[512,512]{1,0:T(8,128)S(1)}, u32[]{:S(2)}) copy-start(f32[512,512]{1,0:T(8,128)S(1)} %get-tuple-element.96) | copy-start | bytes 3145732
  500.2 4.7 copy-start.7
  511.2 1.1 copy-start
  524.2 6.1 %copy-start.2 = (f32[128,3072]{0,1:T(8,128)S(1)}, f32[128,3072]{0,1:T(8,128)}, u32[]{:S(2)}) copy-start(f32[128,3072]{0,1:T(8,128)} %copy.40) | copy-start | bytes 4718596
  531.9 3.2 copy-start.3
  536.7 2.7 copy-start.4
Sparse Core Ops, SparseCore 0:
  159.9 190.3 all-reduce.2
where the time goes:
time: 556 us; the launch traced here: 550 us
  other arithmetic  185 us (33%)
  waiting for transfers between devices  184 us (33%)
  blocking collectives  76.3 us (14%)
  local copies, waits for them, and re-layouts  58.2 us (10%)
  matrix products  24.2 us (4%)
  between operations  17.3 us (3%)
    psum x1, waiting for transfers between devices, local(): gram = lax.psum(local_gram, ('frame', 'tile'))  178 us
    another operation x15, other arithmetic, local(): lower = jnp.linalg.cholesky(gram)  89.5 us
    all_to_all x1, blocking collectives, local(): lax.all_to_all(strain, 'frame', split_axis=3, concat_axis=0, tiled=True)  76.3 us
    another operation x2, other arithmetic, local(): lax.linalg.triangular_solve(lower, snapshot, left_side=True, lower=True)  41 us
    select_n x1, other arithmetic, derivative(): jnp.where(first, after - center, jnp.where(final, center - before, (after...  22.9 us
    another operation x7, matrix products, local(): lax.linalg.triangular_solve(lower, snapshot, left_side=True, lower=True)  19.5 us
    another operation x9, local copies, waits for them, and re-layouts, local(): lax.linalg.triangular_solve(lower, snapshot, left_side=True, lower=True)  16.8 us
    unnamed x19, local copies, waits for them, and re-layouts  16.4 us
  transfers between devices with their start and end apart: 3, of which 3 were waited for; matrix products, arithmetic and copies ran while one was open for 2% of the time, Pallas kernels for 0%

commit v1 on v0

v1 whole, which is shorter than its diff:
```python
import functools
import math

import jax
import jax.numpy as jnp
from jax import lax
from jax.experimental import pallas as pl
from jax.experimental.pallas import tpu as pltpu
from jax.sharding import PartitionSpec as P

MESH = pl.DeviceIdType.MESH
BLOCK = 128
NT = (((1,), (1,)), ((), ()))
TN = (((0,), (0,)), ((), ()))
EXACT = lax.Precision.HIGHEST


def sum_stages(nz, nt, rows):
    stages = []
    for axis, peers in (("tile", nt), ("frame", nz)):
        distance = 1
        while distance < peers:
            halved = rows % 16 == 0
            rows = rows // 2 if halved else rows
            stages.append((axis, distance, rows, halved))
            distance *= 2
    return stages


def exchange_kernel(nz, nt, stages, x_ref, gram_ref, s_ref, center, above, below, edge_out, edge_in,
                    edge_cols, acc, landing, total, own_sem, a2a_send, a2a_recv, edge_send, edge_recv,
                    up_send, up_recv, dn_send, dn_recv, sum_send, sum_recv):
    z, t = lax.axis_index("frame"), lax.axis_index("tile")
    fb, wb = x_ref.shape[1], x_ref.shape[2] // nz
    frames = fb * nz

    barrier = pltpu.get_barrier_semaphore()
    greeted = 0
    for k in range(1, nz):
        pl.semaphore_signal(barrier, inc=1, device_id={"frame": lax.rem(z + k, nz)}, device_id_type=MESH)
        greeted += 1
    for k in (1, nt - 1):
        pl.semaphore_signal(barrier, inc=1, device_id={"tile": lax.rem(t + k, nt)}, device_id_type=MESH)
        greeted += 1
    distance = 2
    while distance < nt:
        peer = t + distance * (1 - 2 * ((t // distance) % 2))
        pl.semaphore_signal(barrier, inc=1, device_id={"tile": peer}, device_id_type=MESH)
        greeted += 1
        distance *= 2
    pl.semaphore_wait(barrier, greeted)

    own = pltpu.make_async_copy(
        x_ref.at[:, :, pl.ds(pl.multiple_of(z * wb, 128), wb)],
        center.at[:, pl.ds(pl.multiple_of(z * fb, 16), fb), :], own_sem)
    own.start()
    blocks = [None]
    for k in range(1, nz):
        d = lax.rem(z + k, nz)
        copy = pltpu.make_async_remote_copy(
            src_ref=x_ref.at[:, :, pl.ds(pl.multiple_of(d * wb, 128), wb)],
            dst_ref=center.at[:, pl.ds(pl.multiple_of(z * fb, 16), fb), :],
            send_sem=a2a_send.at[k], recv_sem=a2a_recv.at[k],
            device_id={"frame": d}, device_id_type=MESH)
        copy.start()
        blocks.append(copy)

    row16 = lax.broadcasted_iota(jnp.int32, (16, 128), 0)
    lane16 = lax.broadcasted_iota(jnp.int32, (16, 128), 1)

    def pick(row, lane):
        return jnp.where((row16 == row) & (lane16 == lane), 1.0, 0.0).astype(jnp.bfloat16)

    for d in range(nz):
        total_edge = jnp.zeros((16, fb), jnp.float32)
        for c in range(2):
            if d > 0:
                total_edge += lax.dot_general(pick(2 * c, 127), x_ref[c, :, d * wb - 128:d * wb], NT,
                                              preferred_element_type=jnp.float32)
            if d < nz - 1:
                total_edge += lax.dot_general(pick(2 * c + 1, 0), x_ref[c, :, (d + 1) * wb:(d + 1) * wb + 128], NT,
                                              preferred_element_type=jnp.float32)
        edge_out[d] = total_edge.astype(jnp.bfloat16)
    edges = [None]
    for k in range(1, nz):
        d = lax.rem(z + k, nz)
        copy = pltpu.make_async_remote_copy(
            src_ref=edge_out.at[d], dst_ref=edge_in.at[z],
            send_sem=edge_send.at[k], recv_sem=edge_recv.at[k],
            device_id={"frame": d}, device_id_type=MESH)
        copy.start()
        edges.append(copy)
    edge_in[z] = edge_out[z]

    halos = []
    for k in range(nz):
        if k == 0:
            own.wait()
        else:
            blocks[k].wait_recv()
        s = lax.rem(z - k + nz, nz)
        rows = pl.ds(pl.multiple_of(s * fb, 16), fb)
        up = pltpu.make_async_remote_copy(
            src_ref=center.at[:, rows, :], dst_ref=above.at[:, rows, :],
            send_sem=up_send.at[k], recv_sem=up_recv.at[k],
            device_id={"tile": lax.rem(t + 1, nt)}, device_id_type=MESH)
        dn = pltpu.make_async_remote_copy(
            src_ref=center.at[:, rows, :], dst_ref=below.at[:, rows, :],
            send_sem=dn_send.at[k], recv_sem=dn_recv.at[k],
            device_id={"tile": lax.rem(t + nt - 1, nt)}, device_id_type=MESH)
        halos.append((up, dn, s))

        @pl.when(t < nt - 1)
        def _(up=up):
            up.start()

        @pl.when(t > 0)
        def _(dn=dn):
            dn.start()

    lane = lax.broadcasted_iota(jnp.int32, (16, wb), 1)
    outer_first, outer_last = (z == 0), (z == nz - 1)
    at_first, at_last = lane == 0, lane == wb - 1
    col_scale = jnp.where((at_first & outer_first) | (at_last & outer_last), 1.0, 0.5)
    row_scale = jnp.where((t == 0) | (t == nt - 1), 1.0, 0.5)
    eye = jnp.where(row16 == lane16, 1.0, 0.0).astype(jnp.bfloat16)

    for k in range(nz):
        up, dn, s = halos[k]
        base = s * fb

        @pl.when(t > 0)
        def _(up=up):
            up.wait_recv()

        @pl.when(t < nt - 1)
        def _(dn=dn):
            dn.wait_recv()

        rows = pl.ds(pl.multiple_of(base, 16), fb)

        @pl.when(t == 0)
        def _(rows=rows):
            above[:, rows, :] = center[:, rows, :]

        @pl.when(t == nt - 1)
        def _(rows=rows):
            below[:, rows, :] = center[:, rows, :]

        if k > 0:
            edges[k].wait_recv()
        edge_cols[...] = lax.dot_general(edge_in[s], eye, TN, preferred_element_type=jnp.float32)

        def body(i, carry, base=base):
            at = pl.ds(pl.multiple_of(base + i * 16, 16), 16)
            cols = edge_cols[pl.ds(pl.multiple_of(i * 16, 16), 16), :]

            def column(f, c):
                before = jnp.where(at_first, jnp.where(outer_first, f, cols[:, 2 * c:2 * c + 1]), pltpu.roll(f, 1, 1))
                after = jnp.where(at_last, jnp.where(outer_last, f, cols[:, 2 * c + 1:2 * c + 2]),
                                  pltpu.roll(f, wb - 1, 1))
                return (after - before) * col_scale

            def row(c):
                return (below[c, at, :].astype(jnp.float32) - above[c, at, :].astype(jnp.float32)) * row_scale

            s_ref[0, at, :] = column(center[0, at, :].astype(jnp.float32), 0).astype(jnp.bfloat16)
            s_ref[1, at, :] = row(1).astype(jnp.bfloat16)
            s_ref[2, at, :] = (0.5 * (row(0) + column(center[1, at, :].astype(jnp.float32), 1))).astype(jnp.bfloat16)
            return carry

        lax.fori_loop(0, fb // 16, body, 0)

    index = 0
    for i in range(frames // BLOCK):
        width = (i + 1) * BLOCK
        part = jnp.zeros((BLOCK, width), jnp.float32)
        for c in range(3):
            part += lax.dot_general(s_ref[c, i * BLOCK:(i + 1) * BLOCK, :], s_ref[c, :width, :], NT,
                                    preferred_element_type=jnp.float32)
        for j in range(i + 1):
            acc[index * BLOCK:(index + 1) * BLOCK, :] = part[:, j * BLOCK:(j + 1) * BLOCK]
            index += 1

    lo, place, waits, trail = 0, 0, [], []
    for n, (axis, distance, size, halved) in enumerate(stages):
        me = z if axis == "frame" else t
        bit = (me // distance) % 2
        peer = me + distance * (1 - 2 * bit)
        keep = lo + bit * size if halved else lo
        give = lo + (1 - bit) * size if halved else lo
        copy = pltpu.make_async_remote_copy(
            src_ref=acc.at[pl.ds(pl.multiple_of(give, 8), size), :], dst_ref=landing.at[place:place + size, :],
            send_sem=sum_send.at[n], recv_sem=sum_recv.at[n],
            device_id={axis: peer}, device_id_type=MESH)
        copy.start()
        copy.wait()
        at = pl.ds(pl.multiple_of(keep, 8), size)
        acc[at, :] = acc[at, :] + landing[place:place + size, :]
        if halved:
            trail.append((axis, peer, size, keep, lo))
        lo = keep
        place += size
    size = stages[-1][2]
    at = pl.ds(pl.multiple_of(lo, 8), size)
    total[at, :] = acc[at, :]
    for m, (axis, peer, size, keep, lo) in enumerate(reversed(trail)):
        n = len(stages) + m
        at = pl.ds(pl.multiple_of(keep, 8), size)
        copy = pltpu.make_async_remote_copy(
            src_ref=total.at[at, :], dst_ref=total.at[at, :],
            send_sem=sum_send.at[n], recv_sem=sum_recv.at[n],
            device_id={axis: peer}, device_id_type=MESH)
        copy.start()
        copy.wait()
    gram_ref[...] = total[...]

    for k in range(nz):
        up, dn, _ = halos[k]
        if k > 0:
            blocks[k].wait_send()
            edges[k].wait_send()

        @pl.when(t < nt - 1)
        def _(up=up):
            up.wait_send()

        @pl.when(t > 0)
        def _(dn=dn):
            dn.wait_send()


def exchange(x, nz, nt):
    fb, width = x.shape[1], x.shape[2]
    wb, frames = width // nz, fb * nz
    nb = frames // BLOCK
    rows = nb * (nb + 1) // 2 * BLOCK
    stages = sum_stages(nz, nt, rows)
    landing = sum(stage[2] for stage in stages)
    dma = pltpu.SemaphoreType.DMA
    vmem = pl.BlockSpec(memory_space=pltpu.VMEM)
    return pl.pallas_call(
        functools.partial(exchange_kernel, nz, nt, stages),
        out_shape=(jax.ShapeDtypeStruct((rows, BLOCK), jnp.float32),
                   jax.ShapeDtypeStruct((3, frames, wb), jnp.bfloat16)),
        in_specs=[vmem],
        out_specs=(vmem, vmem),
        scratch_shapes=[
            pltpu.VMEM((2, frames, wb), jnp.bfloat16),
            pltpu.VMEM((2, frames, wb), jnp.bfloat16),
            pltpu.VMEM((2, frames, wb), jnp.bfloat16),
            pltpu.VMEM((nz, 16, fb), jnp.bfloat16),
            pltpu.VMEM((nz, 16, fb), jnp.bfloat16),
            pltpu.VMEM((fb, 128), jnp.float32),
            pltpu.VMEM((rows, BLOCK), jnp.float32),
            pltpu.VMEM((landing, BLOCK), jnp.float32),
            pltpu.VMEM((rows, BLOCK), jnp.float32),
            dma, dma((nz,)), dma((nz,)), dma((nz,)), dma((nz,)),
            dma((nz,)), dma((nz,)), dma((nz,)), dma((nz,)),
            dma((2 * len(stages),)), dma((2 * len(stages),)),
        ],
        compiler_params=pltpu.CompilerParams(
            collective_id=0, has_side_effects=True, vmem_limit_bytes=40 * 1024 * 1024),
    )(x)


def factor_block(a):
    n = a.shape[0]
    row8 = lax.broadcasted_iota(jnp.int32, (8, n), 0)
    lane8 = lax.broadcasted_iota(jnp.int32, (8, n), 1)
    left = [a[8 * i:8 * i + 8, :] for i in range(n // 8)]
    right = [jnp.where(row8 + 8 * i == lane8, 1.0, 0.0) for i in range(n // 8)]
    for j in range(n):
        home, sub = j // 8, j % 8
        pivot = jnp.broadcast_to(left[home][sub:sub + 1, j:j + 1], (8, n))
        r = lax.rsqrt(pivot)
        u = jnp.broadcast_to(left[home][sub:sub + 1, :], (8, n)) * r
        m = jnp.broadcast_to(right[home][sub:sub + 1, :], (8, n)) * r
        for i in range(home, n // 8):
            c = jnp.broadcast_to(left[i][:, j:j + 1], (8, n)) * r
            new_left, new_right = left[i] - c * u, right[i] - c * m
            if i == home:
                new_left = jnp.where(row8 > sub, new_left, jnp.where(row8 == sub, u, left[i]))
                new_right = jnp.where(row8 > sub, new_right, jnp.where(row8 == sub, m, right[i]))
            left[i], right[i] = new_left, new_right
    return jnp.concatenate(left, axis=0), jnp.concatenate(right, axis=0)


def basis_kernel(scale, g_ref, s_ref, basis_ref, factor_ref, work, high, low):
    n = factor_ref.shape[0]
    nb = n // BLOCK
    row = lax.broadcasted_iota(jnp.int32, (BLOCK, BLOCK), 0)
    col = lax.broadcasted_iota(jnp.int32, (BLOCK, BLOCK), 1)

    work[...] = jnp.zeros_like(work)
    index = 0
    for i in range(nb):
        for j in range(i + 1):
            block = g_ref[index * BLOCK:(index + 1) * BLOCK, :]
            work[j, :, i * BLOCK:(i + 1) * BLOCK] = block.T
            index += 1
        work[i, :, n + i * BLOCK:n + (i + 1) * BLOCK] = jnp.where(row == col, 1.0, 0.0)

    def step(k, carry):
        diag = pl.ds(pl.multiple_of(k * BLOCK, BLOCK), BLOCK)
        upper, inverse = factor_block(work[k, :, diag])
        strip = jnp.dot(inverse, work[k], precision=EXACT, preferred_element_type=jnp.float32)
        work[k] = strip
        work[k, :, diag] = jnp.where(row <= col, upper, 0.0)
        for i in range(1, nb):
            @pl.when(i > k)
            def _(i=i):
                work[i] = work[i] - lax.dot_general(
                    work[k, :, i * BLOCK:(i + 1) * BLOCK], work[k], TN, precision=EXACT,
                    preferred_element_type=jnp.float32)
        return carry

    lax.fori_loop(0, nb, step, 0)

    for i in range(nb):
        for j in range(nb):
            at = slice(j * BLOCK, (j + 1) * BLOCK)
            block = work[i, :, at] * (1.0 / scale) if j >= i else jnp.zeros((BLOCK, BLOCK), jnp.float32)
            factor_ref[i * BLOCK:(i + 1) * BLOCK, at] = block
        m = work[i, :, n:2 * n] * scale
        head = m.astype(jnp.bfloat16)
        high[i] = head
        low[i] = (m - head.astype(jnp.float32)).astype(jnp.bfloat16)
    for c in range(3):
        for i in range(nb):
            depth = (i + 1) * BLOCK
            s = s_ref[c, :depth, :]
            value = jnp.dot(high[i, :, :depth], s, preferred_element_type=jnp.float32)
            value += jnp.dot(low[i, :, :depth], s, preferred_element_type=jnp.float32)
            basis_ref[c, i * BLOCK:(i + 1) * BLOCK, :] = value.astype(jnp.bfloat16)


def orthonormal(gram, strain, scale):
    frames = strain.shape[1]
    nb = frames // BLOCK
    vmem = pl.BlockSpec(memory_space=pltpu.VMEM)
    return pl.pallas_call(
        functools.partial(basis_kernel, scale),
        out_shape=(jax.ShapeDtypeStruct(strain.shape, jnp.bfloat16),
                   jax.ShapeDtypeStruct((frames, frames), jnp.float32)),
        in_specs=[vmem, vmem],
        out_specs=(vmem, vmem),
        scratch_shapes=[
            pltpu.VMEM((nb, BLOCK, 2 * frames), jnp.float32),
            pltpu.VMEM((nb, BLOCK, frames), jnp.bfloat16),
            pltpu.VMEM((nb, BLOCK, frames), jnp.bfloat16),
        ],
        compiler_params=pltpu.CompilerParams(vmem_limit_bytes=40 * 1024 * 1024),
    )(gram, strain)


def local(nz, nt, displacement):
    frames, rows, width = displacement.shape[0] * nz, displacement.shape[2] * nt, displacement.shape[3]
    scale = math.sqrt(3 * rows * width)
    x = jnp.transpose(displacement[:, :, 0, :], (1, 0, 2))
    gram, strain = exchange(x, nz, nt)
    basis, factor = orthonormal(gram, strain, scale)
    return jnp.transpose(basis, (1, 0, 2))[:, :, None, :], factor


def solution(mesh):
    return jax.shard_map(
        functools.partial(local, mesh.shape["frame"], mesh.shape["tile"]),
        mesh=mesh,
        in_specs=(P("frame", None, "tile", None),),
        out_specs=(P(None, None, "tile", "frame"), P()),
        check_vma=False,
    )
```

time: 556 us -> 191 us (0.34); the launches traced: 550 us -> 191 us
  Pallas kernels: 0 us -> 187 us
  other arithmetic: 185 us -> 0 us
  waiting for transfers between devices: 184 us -> 0 us
  blocking collectives: 76.3 us -> 0 us
  local copies, waits for them, and re-layouts: 58.2 us -> 2.92 us
  matrix products: 24.2 us -> 0 us
  between operations: 17.3 us -> 0.64 us
    pallas_call x0 -> x2, Pallas kernels: none -> 187 us  [the longest x1 108 us: exchange(): pl.pallas_call(functools.partial(exchange_kernel, nz, nt, stages), out_sh...]
    psum x1 -> x0, waiting for transfers between devices: 178 us -> none  [local(): gram = lax.psum(local_gram, ('frame', 'tile'))]
    another operation x19 -> x0, other arithmetic: 141 us -> none  [the longest x15 89.5 us: local(): lower = jnp.linalg.cholesky(gram)]
    all_to_all x1 -> x0, blocking collectives: 76.3 us -> none  [local(): lax.all_to_all(strain, 'frame', split_axis=3, concat_axis=0, tiled=True)]
    another operation x25 -> x0, local copies, waits for them, and re-layouts: 27.4 us -> none  [the longest x9 16.8 us: local(): lax.linalg.triangular_solve(lower, snapshot, left_side=True, lower=True)]
    select_n x1 -> x0, other arithmetic: 22.9 us -> none  [derivative(): jnp.where(first, after - center, jnp.where(final, center - before, (after...]
    another operation x13 -> x0, matrix products: 21.3 us -> none  [the longest x7 19.5 us: local(): lax.linalg.triangular_solve(lower, snapshot, left_side=True, lower=True)]
    convert_element_type x2 -> x0, other arithmetic: 15 us -> none  [the longest x1 9.62 us: local(): field = padded.astype(jnp.float32)]
  transfers between devices with their start and end apart: 3 -> 0, of which waited for: 3 -> 0; matrix products, arithmetic and copies ran while one was open for 2% -> 0% of each run, Pallas kernels for 0% -> 0%
where the time goes in v1:
time: 191 us
  Pallas kernels  187 us (98%)
  local copies, waits for them, and re-layouts  2.92 us (2%)
    pallas_call x1, Pallas kernels, exchange(): pl.pallas_call(functools.partial(exchange_kernel, nz, nt, stages), out_sh...  108 us
    pallas_call x1, Pallas kernels, orthonormal(): pl.pallas_call(functools.partial(basis_kernel, scale), out_shape=(jax.Sha...  78.8 us

profile of v1, /device:TPU:0, one launch (start us, length us, event | category | flops | bytes accessed | tf_op | source)
XLA Modules:
  0.0 190.7 jit_solution(6357357746514524419)
XLA Ops:
  0.6 2.9 %copy.6 = bf16[128,2,1,4096]{3,0,1,2:T(8,128)(2,1)S(1)} copy(bf16[128,2,1,4096]{3,1,2,0:T(2,128)(2,1)} %param.1) | data formatting | bytes 4194304 | tf_op args[0]
  3.5 108.3 %shard_map.30 = (f32[1280,128]{1,0:T(8,128)S(1)}, bf16[3,512,1024]{2,1,0:T(8,128)(2,1)S(1)}) custom-call(bf16[2,128,4096]{2,1,0:T(8,128)(2,1)S(1)} %bitcast.10), custom_call_target="tpu_custom_call" | custom-call | tf_op jit(solution)/shard_map/pallas_call | solution.py:242
  111.9 78.8 %shard_map.31 = (bf16[3,512,1024]{2,1,0:T(8,128)(2,1)}, f32[512,512]{1,0:T(8,128)}) custom-call(f32[1280,128]{1,0:T(8,128)S(1)} %get-tuple-element.6.g_ref, bf16[3,512,1024]{2,1,0:T(8,128)(2,1)S(1)} %get-tuple-element.7.s_ref), custom_call_target="tpu_custom_call" | custom-call | tf_op jit(solution)/shard_map/pallas_call | solution.py:342

commit v2 on v1

v2 whole, which is shorter than its diff:
```python
import functools
import math

import jax
import jax.numpy as jnp
from jax import lax
from jax.experimental import pallas as pl
from jax.experimental.pallas import tpu as pltpu
from jax.sharding import PartitionSpec as P

MESH = pl.DeviceIdType.MESH
BLOCK = 128
PIECES = 4
GROUP = 8
NT = (((1,), (1,)), ((), ()))
TN = (((0,), (0,)), ((), ()))
EXACT = lax.Precision.HIGHEST


def sum_stages(nz, nt, rows):
    stages = []
    for name, peers in (("core", 2), ("chip", nt // 2), ("frame", nz)):
        split = rows % (8 * peers) == 0
        rows = rows // peers if split else rows
        stages.append((name, peers, rows, split))
    return stages


def exchange_kernel(nz, nt, stages, x_ref, gram_ref, s_ref, center, above, below, edge_out, edge_in,
                    edge_cols, acc, landing, total, own_sem, a2a_send, a2a_recv, edge_send, edge_recv,
                    up_send, up_recv, dn_send, dn_recv, sum_send, sum_recv):
    z, t = lax.axis_index("frame"), lax.axis_index("tile")
    fb, wb = x_ref.shape[1], x_ref.shape[2] // nz
    frames, part = fb * nz, fb // PIECES
    chips = nt // 2
    core, chip = t % 2, t // 2

    def member(name, k):
        if name == "core":
            return core, lax.rem(core + k, 2), {"tile": chip * 2 + lax.rem(core + k, 2)}
        if name == "chip":
            return chip, lax.rem(chip + k, chips), {"tile": lax.rem(chip + k, chips) * 2 + core}
        return z, lax.rem(z + k, nz), {"frame": lax.rem(z + k, nz)}

    barrier = pltpu.get_barrier_semaphore()
    greeted = 0
    for name, peers in (("core", 2), ("chip", chips), ("frame", nz)):
        for k in range(1, peers):
            pl.semaphore_signal(barrier, inc=1, device_id=member(name, k)[2], device_id_type=MESH)
            greeted += 1
    for k in (1, nt - 1):
        pl.semaphore_signal(barrier, inc=1, device_id={"tile": lax.rem(t + k, nt)}, device_id_type=MESH)
        greeted += 1
    pl.semaphore_wait(barrier, greeted)

    def frame_rows(s, p):
        return pl.ds(pl.multiple_of(s * fb + p * part, 16), part)

    own_cols = pl.ds(pl.multiple_of(z * wb, 128), wb)
    own = pltpu.make_async_copy(
        x_ref.at[:, :, own_cols], center.at[:, pl.ds(pl.multiple_of(z * fb, 16), fb), :], own_sem)
    own.start()
    blocks = {}

    def send_piece(p):
        for k in range(1, nz):
            d = lax.rem(z + k, nz)
            copy = pltpu.make_async_remote_copy(
                src_ref=x_ref.at[:, p * part:(p + 1) * part, pl.ds(pl.multiple_of(d * wb, 128), wb)],
                dst_ref=center.at[:, frame_rows(z, p), :],
                send_sem=a2a_send.at[k, p], recv_sem=a2a_recv.at[k, p],
                device_id={"frame": d}, device_id_type=MESH)
            copy.start()
            blocks[k, p] = copy

    halos = {}

    def send_halo(k, p):
        s = lax.rem(z - k + nz, nz)
        rows = frame_rows(s, p)
        src = x_ref.at[:, p * part:(p + 1) * part, own_cols] if k == 0 else center.at[:, rows, :]
        up = pltpu.make_async_remote_copy(
            src_ref=src, dst_ref=above.at[:, rows, :],
            send_sem=up_send.at[k, p], recv_sem=up_recv.at[k, p],
            device_id={"tile": lax.rem(t + 1, nt)}, device_id_type=MESH)
        dn = pltpu.make_async_remote_copy(
            src_ref=src, dst_ref=below.at[:, rows, :],
            send_sem=dn_send.at[k, p], recv_sem=dn_recv.at[k, p],
            device_id={"tile": lax.rem(t + nt - 1, nt)}, device_id_type=MESH)
        halos[k, p] = (up, dn, s)

        @pl.when(t < nt - 1)
        def _():
            up.start()

        @pl.when(t > 0)
        def _():
            dn.start()

    send_piece(0)
    for p in range(PIECES):
        send_halo(0, p)

    row16 = lax.broadcasted_iota(jnp.int32, (16, 128), 0)
    lane16 = lax.broadcasted_iota(jnp.int32, (16, 128), 1)

    def pick(row, lane):
        return jnp.where((row16 == row) & (lane16 == lane), 1.0, 0.0).astype(jnp.bfloat16)

    for d in range(nz):
        total_edge = jnp.zeros((16, fb), jnp.float32)
        for c in range(2):
            if d > 0:
                total_edge += lax.dot_general(pick(2 * c, 127), x_ref[c, :, d * wb - 128:d * wb], NT,
                                              preferred_element_type=jnp.float32)
            if d < nz - 1:
                total_edge += lax.dot_general(pick(2 * c + 1, 0), x_ref[c, :, (d + 1) * wb:(d + 1) * wb + 128], NT,
                                              preferred_element_type=jnp.float32)
        edge_out[d] = total_edge.astype(jnp.bfloat16)
    edges = [None]
    for k in range(1, nz):
        d = lax.rem(z + k, nz)
        copy = pltpu.make_async_remote_copy(
            src_ref=edge_out.at[d], dst_ref=edge_in.at[z],
            send_sem=edge_send.at[k], recv_sem=edge_recv.at[k],
            device_id={"frame": d}, device_id_type=MESH)
        copy.start()
        edges.append(copy)
    edge_in[z] = edge_out[z]
    for p in range(1, PIECES):
        send_piece(p)
    own.wait()

    lane = lax.broadcasted_iota(jnp.int32, (16, wb), 1)
    outer_first, outer_last = (z == 0), (z == nz - 1)
    at_first, at_last = lane == 0, lane == wb - 1
    col_scale = jnp.where((at_first & outer_first) | (at_last & outer_last), 1.0, 0.5)
    row_scale = jnp.where((t == 0) | (t == nt - 1), 1.0, 0.5)
    eye = jnp.where(row16 == lane16, 1.0, 0.0).astype(jnp.bfloat16)

    def strain_piece(k, p):
        up, dn, s = halos[k, p]
        rows = frame_rows(s, p)

        @pl.when(t > 0)
        def _():
            up.wait_recv()

        @pl.when(t < nt - 1)
        def _():
            dn.wait_recv()

        @pl.when(t == 0)
        def _():
            above[:, rows, :] = center[:, rows, :]

        @pl.when(t == nt - 1)
        def _():
            below[:, rows, :] = center[:, rows, :]

        if p == 0:
            if k > 0:
                edges[k].wait_recv()
            edge_cols[k] = lax.dot_general(edge_in[s], eye, TN, preferred_element_type=jnp.float32)

        def body(i, carry):
            at = pl.ds(pl.multiple_of(s * fb + p * part + i * 16, 16), 16)
            cols = edge_cols[k, pl.ds(pl.multiple_of(p * part + i * 16, 16), 16), :]

            def column(f, c):
                before = jnp.where(at_first, jnp.where(outer_first, f, cols[:, 2 * c:2 * c + 1]), pltpu.roll(f, 1, 1))
                after = jnp.where(at_last, jnp.where(outer_last, f, cols[:, 2 * c + 1:2 * c + 2]),
                                  pltpu.roll(f, wb - 1, 1))
                return (after - before) * col_scale

            def row(c):
                return (below[c, at, :].astype(jnp.float32) - above[c, at, :].astype(jnp.float32)) * row_scale

            s_ref[0, at, :] = column(center[0, at, :].astype(jnp.float32), 0).astype(jnp.bfloat16)
            s_ref[1, at, :] = row(1).astype(jnp.bfloat16)
            s_ref[2, at, :] = (0.5 * (row(0) + column(center[1, at, :].astype(jnp.float32), 1))).astype(jnp.bfloat16)
            return carry

        lax.fori_loop(0, part // 16, body, 0)

    for p in range(PIECES + 1):
        if p < PIECES:
            for k in range(1, nz):
                blocks[k, p].wait_recv()
                send_halo(k, p)
        if p > 0:
            for k in range(nz):
                strain_piece(k, p - 1)

    index = 0
    for i in range(frames // BLOCK):
        width = (i + 1) * BLOCK
        value = jnp.zeros((BLOCK, width), jnp.float32)
        for c in range(3):
            value += lax.dot_general(s_ref[c, i * BLOCK:(i + 1) * BLOCK, :], s_ref[c, :width, :], NT,
                                     preferred_element_type=jnp.float32)
        for j in range(i + 1):
            acc[index * BLOCK:(index + 1) * BLOCK, :] = value[:, j * BLOCK:(j + 1) * BLOCK]
            index += 1

    lo, place, slot, trail = 0, 0, 0, []
    for name, peers, size, split in stages:
        me = member(name, 0)[0]
        mine = pl.ds(pl.multiple_of(place + me * size, 8), size)
        copies = []
        for k in range(1, peers):
            _, index, device = member(name, k)
            give = lo + index * size if split else lo
            copy = pltpu.make_async_remote_copy(
                src_ref=acc.at[pl.ds(pl.multiple_of(give, 8), size), :], dst_ref=landing.at[mine, :],
                send_sem=sum_send.at[slot], recv_sem=sum_recv.at[slot],
                device_id=device, device_id_type=MESH)
            copy.start()
            copies.append(copy)
            slot += 1
        keep = lo + me * size if split else lo
        at = pl.ds(pl.multiple_of(keep, 8), size)
        landing[mine, :] = acc[at, :]
        for copy in copies:
            copy.wait()
        value = landing[place:place + size, :]
        for n in range(1, peers):
            value += landing[place + n * size:place + (n + 1) * size, :]
        acc[at, :] = value
        if split:
            trail.append((name, peers, size, keep))
        lo = keep
        place += peers * size
    at = pl.ds(pl.multiple_of(lo, 8), stages[-1][2])
    total[at, :] = acc[at, :]
    for name, peers, size, keep in reversed(trail):
        at = pl.ds(pl.multiple_of(keep, 8), size)
        copies = []
        for k in range(1, peers):
            copy = pltpu.make_async_remote_copy(
                src_ref=total.at[at, :], dst_ref=total.at[at, :],
                send_sem=sum_send.at[slot], recv_sem=sum_recv.at[slot],
                device_id=member(name, k)[2], device_id_type=MESH)
            copy.start()
            copies.append(copy)
            slot += 1
        for copy in copies:
            copy.wait()
    gram_ref[...] = total[...]

    for k in range(1, nz):
        edges[k].wait_send()
    for k in range(nz):
        for p in range(PIECES):
            up, dn, _ = halos[k, p]
            if k > 0:
                blocks[k, p].wait_send()

            @pl.when(t < nt - 1)
            def _(up=up):
                up.wait_send()

            @pl.when(t > 0)
            def _(dn=dn):
                dn.wait_send()


def exchange(x, nz, nt):
    fb, width = x.shape[1], x.shape[2]
    wb, frames = width // nz, fb * nz
    nb = frames // BLOCK
    rows = nb * (nb + 1) // 2 * BLOCK
    stages = sum_stages(nz, nt, rows)
    landing = sum(stage[1] * stage[2] for stage in stages)
    steps = 2 * sum(stage[1] - 1 for stage in stages)
    dma = pltpu.SemaphoreType.DMA
    vmem = pl.BlockSpec(memory_space=pltpu.VMEM)
    return pl.pallas_call(
        functools.partial(exchange_kernel, nz, nt, stages),
        out_shape=(jax.ShapeDtypeStruct((rows, BLOCK), jnp.float32),
                   jax.ShapeDtypeStruct((3, frames, wb), jnp.bfloat16)),
        in_specs=[vmem],
        out_specs=(vmem, vmem),
        scratch_shapes=[
            pltpu.VMEM((2, frames, wb), jnp.bfloat16),
            pltpu.VMEM((2, frames, wb), jnp.bfloat16),
            pltpu.VMEM((2, frames, wb), jnp.bfloat16),
            pltpu.VMEM((nz, 16, fb), jnp.bfloat16),
            pltpu.VMEM((nz, 16, fb), jnp.bfloat16),
            pltpu.VMEM((nz, fb, 128), jnp.float32),
            pltpu.VMEM((rows, BLOCK), jnp.float32),
            pltpu.VMEM((landing, BLOCK), jnp.float32),
            pltpu.VMEM((rows, BLOCK), jnp.float32),
            dma, dma((nz, PIECES)), dma((nz, PIECES)), dma((nz,)), dma((nz,)),
            dma((nz, PIECES)), dma((nz, PIECES)), dma((nz, PIECES)), dma((nz, PIECES)),
            dma((steps,)), dma((steps,)),
        ],
        compiler_params=pltpu.CompilerParams(
            collective_id=0, has_side_effects=True, vmem_limit_bytes=40 * 1024 * 1024),
    )(x)


def factor_block(a):
    n = a.shape[0]
    shape = (GROUP, n)
    row8 = lax.broadcasted_iota(jnp.int32, shape, 0)
    lane8 = lax.broadcasted_iota(jnp.int32, shape, 1)
    tiles = n // GROUP
    left = [a[GROUP * i:GROUP * (i + 1), :] for i in range(tiles)]
    right = [jnp.where(row8 + GROUP * i == lane8, 1.0, 0.0) for i in range(tiles)]

    def row_of(tile, p):
        return jnp.broadcast_to(tile[p:p + 1, :], shape)

    for g in range(tiles):
        first = GROUP * g
        columns = [jnp.broadcast_to(left[g][:, first + q:first + q + 1], shape) for q in range(GROUP)]
        entry = {(p, q): row_of(columns[q], p) for p in range(GROUP) for q in range(p + 1)}
        r = []
        for q in range(GROUP):
            r.append(lax.rsqrt(entry[q, q]))
            for p in range(q + 1, GROUP):
                entry[p, q] = entry[p, q] * r[q]
            for p in range(q + 1, GROUP):
                for m in range(q + 1, p + 1):
                    entry[p, m] = entry[p, m] - entry[p, q] * entry[m, q]
        tops = []
        for tile in (left[g], right[g]):
            rows = [row_of(tile, p) for p in range(GROUP)]
            for q in range(GROUP):
                rows[q] = rows[q] * r[q]
                for p in range(q + 1, GROUP):
                    rows[p] = rows[p] - entry[p, q] * rows[q]
            tops.append(rows)
        for i in range(g + 1, tiles):
            c = [jnp.broadcast_to(left[i][:, first + q:first + q + 1], shape) for q in range(GROUP)]
            for q in range(GROUP):
                c[q] = c[q] * r[q]
                for m in range(q + 1, GROUP):
                    c[m] = c[m] - c[q] * entry[m, q]
            for q in range(GROUP):
                left[i] = left[i] - c[q] * tops[0][q]
                right[i] = right[i] - c[q] * tops[1][q]
        packed = []
        for rows in tops:
            value = rows[0]
            for q in range(1, GROUP):
                value = jnp.where(row8 == q, rows[q], value)
            packed.append(value)
        left[g], right[g] = packed
    return jnp.concatenate(left, axis=0), jnp.concatenate(right, axis=0)


def basis_kernel(scale, g_ref, s_ref, basis_ref, factor_ref, work, planes):
    n = factor_ref.shape[0]
    wide = n // 2
    nb = n // BLOCK
    row = lax.broadcasted_iota(jnp.int32, (BLOCK, BLOCK), 0)
    col = lax.broadcasted_iota(jnp.int32, (BLOCK, BLOCK), 1)

    work[...] = jnp.zeros_like(work)
    index = 0
    for i in range(nb):
        for j in range(i + 1):
            block = g_ref[index * BLOCK:(index + 1) * BLOCK, :]
            work[j, :, i * BLOCK:(i + 1) * BLOCK] = block.T
            index += 1
        work[i, :, n + i * BLOCK:n + (i + 1) * BLOCK] = jnp.where(row == col, 1.0, 0.0)

    def step(k, carry):
        diag = pl.ds(pl.multiple_of(k * BLOCK, BLOCK), BLOCK)
        upper, inverse = factor_block(work[k, :, diag])
        window = pl.ds(pl.multiple_of(k * BLOCK, BLOCK), n + BLOCK)
        strip = jnp.dot(inverse, work[k, :, window], precision=EXACT, preferred_element_type=jnp.float32)
        work[k, :, window] = strip
        work[k, :, diag] = jnp.where(row <= col, upper, 0.0)
        for i in range(1, nb):
            @pl.when(i > k)
            def _(i=i):
                work[i, :, window] = work[i, :, window] - lax.dot_general(
                    work[k, :, i * BLOCK:(i + 1) * BLOCK], work[k, :, window], TN, precision=EXACT,
                    preferred_element_type=jnp.float32)
        return carry

    lax.fori_loop(0, nb, step, 0)

    for i in range(nb):
        for j in range(nb):
            at = slice(j * BLOCK, (j + 1) * BLOCK)
            block = work[i, :, at] * (1.0 / scale) if j >= i else jnp.zeros((BLOCK, BLOCK), jnp.float32)
            factor_ref[i * BLOCK:(i + 1) * BLOCK, at] = block
        m = work[i, :, n:2 * n] * scale
        head = m.astype(jnp.bfloat16)
        half, at = i * BLOCK // wide, (i * BLOCK) % wide
        planes[half, at:at + BLOCK, :] = head
        planes[half, wide + at:wide + at + BLOCK, :] = (m - head.astype(jnp.float32)).astype(jnp.bfloat16)
    for c in range(3):
        for i in range(n // wide):
            depth = (i + 1) * wide
            value = jnp.dot(planes[i, :, :depth], s_ref[c, :depth, :], preferred_element_type=jnp.float32)
            basis_ref[c, i * wide:(i + 1) * wide, :] = (value[:wide] + value[wide:]).astype(jnp.bfloat16)


def orthonormal(gram, strain, scale):
    frames = strain.shape[1]
    nb = frames // BLOCK
    vmem = pl.BlockSpec(memory_space=pltpu.VMEM)
    return pl.pallas_call(
        functools.partial(basis_kernel, scale),
        out_shape=(jax.ShapeDtypeStruct(strain.shape, jnp.bfloat16),
                   jax.ShapeDtypeStruct((frames, frames), jnp.float32)),
        in_specs=[vmem, vmem],
        out_specs=(vmem, vmem),
        scratch_shapes=[
            pltpu.VMEM((nb, BLOCK, 2 * frames), jnp.float32),
            pltpu.VMEM((2, frames, frames), jnp.bfloat16),
        ],
        compiler_params=pltpu.CompilerParams(vmem_limit_bytes=40 * 1024 * 1024),
    )(gram, strain)


def local(nz, nt, displacement):
    frames, rows, width = displacement.shape[0] * nz, displacement.shape[2] * nt, displacement.shape[3]
    scale = math.sqrt(3 * rows * width)
    x = jnp.transpose(displacement[:, :, 0, :], (1, 0, 2))
    gram, strain = exchange(x, nz, nt)
    basis, factor = orthonormal(gram, strain, scale)
    return jnp.transpose(basis, (1, 0, 2))[:, :, None, :], factor


def solution(mesh):
    return jax.shard_map(
        functools.partial(local, mesh.shape["frame"], mesh.shape["tile"]),
        mesh=mesh,
        in_specs=(P("frame", None, "tile", None),),
        out_specs=(P(None, None, "tile", "frame"), P()),
        check_vma=False,
    )
```

time: 191 us -> 117 us (0.61)
  Pallas kernels: 187 us -> 114 us
    pallas_call x1, Pallas kernels: 78.8 us -> 27.7 us  [orthonormal(): pl.pallas_call(functools.partial(basis_kernel, scale), out_shape=(jax.Sha...]
    pallas_call x1, Pallas kernels: 108 us -> 86 us  [exchange(): pl.pallas_call(functools.partial(exchange_kernel, nz, nt, stages), out_sh...]
where the time goes in v2:
time: 117 us
  Pallas kernels  114 us (97%)
  local copies, waits for them, and re-layouts  2.92 us (2%)
    pallas_call x1, Pallas kernels, exchange(): pl.pallas_call(functools.partial(exchange_kernel, nz, nt, stages), out_sh...  86 us
    pallas_call x1, Pallas kernels, orthonormal(): pl.pallas_call(functools.partial(basis_kernel, scale), out_shape=(jax.Sha...  27.7 us
    unnamed x1, local copies, waits for them, and re-layouts  2.92 us

profile of v2, /device:TPU:0, one launch (start us, length us, event | category | flops | bytes accessed | tf_op | source)
XLA Modules:
  0.0 117.3 jit_solution(2425484826568245588)
XLA Ops:
  0.6 2.9 %copy.6 = bf16[128,2,1,4096]{3,0,1,2:T(8,128)(2,1)S(1)} copy(bf16[128,2,1,4096]{3,1,2,0:T(2,128)(2,1)} %param.1) | data formatting | bytes 4194304 | tf_op args[0]
  3.5 86.0 %shard_map.30 = (f32[1280,128]{1,0:T(8,128)S(1)}, bf16[3,512,1024]{2,1,0:T(8,128)(2,1)S(1)}) custom-call(bf16[2,128,4096]{2,1,0:T(8,128)(2,1)S(1)} %bitcast.10), custom_call_target="tpu_custom_call" | custom-call | tf_op jit(solution)/shard_map/pallas_call | solution.py:278
  89.6 27.7 %shard_map.31 = (bf16[3,512,1024]{2,1,0:T(8,128)(2,1)}, f32[512,512]{1,0:T(8,128)}) custom-call(f32[1280,128]{1,0:T(8,128)S(1)} %get-tuple-element.6.g_ref, bf16[3,512,1024]{2,1,0:T(8,128)(2,1)S(1)} %get-tuple-element.7.s_ref), custom_call_target="tpu_custom_call" | custom-call | tf_op jit(solution)/shard_map/pallas_call | solution.py:408

commit v3 on v2

--- a/solution.py
+++ b/solution.py
@@ -10,7 +10,8 @@
 
 MESH = pl.DeviceIdType.MESH
 BLOCK = 128
-PIECES = 4
+PIECE = 16
+AHEAD = 3
 GROUP = 8
 NT = (((1,), (1,)), ((), ()))
 TN = (((0,), (0,)), ((), ()))
@@ -31,7 +32,7 @@
                     up_send, up_recv, dn_send, dn_recv, sum_send, sum_recv):
     z, t = lax.axis_index("frame"), lax.axis_index("tile")
     fb, wb = x_ref.shape[1], x_ref.shape[2] // nz
-    frames, part = fb * nz, fb // PIECES
+    frames, part, pieces = fb * nz, PIECE, fb // PIECE
     chips = nt // 2
     core, chip = t % 2, t // 2
 
@@ -97,38 +98,41 @@
         def _():
             dn.start()
 
-    send_piece(0)
-    for p in range(PIECES):
-        send_halo(0, p)
-
     row16 = lax.broadcasted_iota(jnp.int32, (16, 128), 0)
     lane16 = lax.broadcasted_iota(jnp.int32, (16, 128), 1)
 
     def pick(row, lane):
         return jnp.where((row16 == row) & (lane16 == lane), 1.0, 0.0).astype(jnp.bfloat16)
 
-    for d in range(nz):
-        total_edge = jnp.zeros((16, fb), jnp.float32)
-        for c in range(2):
-            if d > 0:
-                total_edge += lax.dot_general(pick(2 * c, 127), x_ref[c, :, d * wb - 128:d * wb], NT,
-                                              preferred_element_type=jnp.float32)
-            if d < nz - 1:
-                total_edge += lax.dot_general(pick(2 * c + 1, 0), x_ref[c, :, (d + 1) * wb:(d + 1) * wb + 128], NT,
-                                              preferred_element_type=jnp.float32)
-        edge_out[d] = total_edge.astype(jnp.bfloat16)
     edges = [None]
-    for k in range(1, nz):
-        d = lax.rem(z + k, nz)
-        copy = pltpu.make_async_remote_copy(
-            src_ref=edge_out.at[d], dst_ref=edge_in.at[z],
-            send_sem=edge_send.at[k], recv_sem=edge_recv.at[k],
-            device_id={"frame": d}, device_id_type=MESH)
-        copy.start()
-        edges.append(copy)
-    edge_in[z] = edge_out[z]
-    for p in range(1, PIECES):
+
+    def send_edges():
+        for d in range(nz):
+            total_edge = jnp.zeros((16, fb), jnp.float32)
+            for c in range(2):
+                if d > 0:
+                    total_edge += lax.dot_general(pick(2 * c, 127), x_ref[c, :, d * wb - 128:d * wb], NT,
+                                                  preferred_element_type=jnp.float32)
+                if d < nz - 1:
+                    total_edge += lax.dot_general(pick(2 * c + 1, 0), x_ref[c, :, (d + 1) * wb:(d + 1) * wb + 128], NT,
+                                                  preferred_element_type=jnp.float32)
+            edge_out[d] = total_edge.astype(jnp.bfloat16)
+        for k in range(1, nz):
+            d = lax.rem(z + k, nz)
+            copy = pltpu.make_async_remote_copy(
+                src_ref=edge_out.at[d], dst_ref=edge_in.at[z],
+                send_sem=edge_send.at[k], recv_sem=edge_recv.at[k],
+                device_id={"frame": d}, device_id_type=MESH)
+            copy.start()
+            edges.append(copy)
+        edge_in[z] = edge_out[z]
+
+    for p in range(min(AHEAD, pieces)):
         send_piece(p)
+        send_halo(0, p)
+        if p == 0:
+            send_edges()
+
     own.wait()
 
     lane = lax.broadcasted_iota(jnp.int32, (16, wb), 1)
@@ -138,34 +142,34 @@
     row_scale = jnp.where((t == 0) | (t == nt - 1), 1.0, 0.5)
     eye = jnp.where(row16 == lane16, 1.0, 0.0).astype(jnp.bfloat16)
 
-    def strain_piece(k, p):
-        up, dn, s = halos[k, p]
-        rows = frame_rows(s, p)
-
-        @pl.when(t > 0)
-        def _():
-            up.wait_recv()
-
-        @pl.when(t < nt - 1)
-        def _():
-            dn.wait_recv()
-
-        @pl.when(t == 0)
-        def _():
-            above[:, rows, :] = center[:, rows, :]
-
-        @pl.when(t == nt - 1)
-        def _():
-            below[:, rows, :] = center[:, rows, :]
-
-        if p == 0:
-            if k > 0:
-                edges[k].wait_recv()
-            edge_cols[k] = lax.dot_general(edge_in[s], eye, TN, preferred_element_type=jnp.float32)
-
-        def body(i, carry):
-            at = pl.ds(pl.multiple_of(s * fb + p * part + i * 16, 16), 16)
-            cols = edge_cols[k, pl.ds(pl.multiple_of(p * part + i * 16, 16), 16), :]
+    def strain_piece(p):
+        for k in range(nz):
+            up, dn, s = halos[k, p]
+
+            @pl.when(t > 0)
+            def _(up=up):
+                up.wait_recv()
+
+            @pl.when(t < nt - 1)
+            def _(dn=dn):
+                dn.wait_recv()
+
+            if p == 0:
+                if k > 0:
+                    edges[k].wait_recv()
+                edge_cols[k] = lax.dot_general(edge_in[s], eye, TN, preferred_element_type=jnp.float32)
+
+        def body(k, carry):
+            at = frame_rows(lax.rem(z - k + nz, nz), p)
+            cols = edge_cols[k, p * part:(p + 1) * part, :]
+
+            @pl.when(t == 0)
+            def _():
+                above[:, at, :] = center[:, at, :]
+
+            @pl.when(t == nt - 1)
+            def _():
+                below[:, at, :] = center[:, at, :]
 
             def column(f, c):
                 before = jnp.where(at_first, jnp.where(outer_first, f, cols[:, 2 * c:2 * c + 1]), pltpu.roll(f, 1, 1))
@@ -181,27 +185,46 @@
             s_ref[2, at, :] = (0.5 * (row(0) + column(center[1, at, :].astype(jnp.float32), 1))).astype(jnp.bfloat16)
             return carry
 
-        lax.fori_loop(0, part // 16, body, 0)
-
-    for p in range(PIECES + 1):
-        if p < PIECES:
+        lax.fori_loop(0, nz, body, 0)
+
+    for p in range(pieces + 1):
+        if p < pieces:
             for k in range(1, nz):
                 blocks[k, p].wait_recv()
                 send_halo(k, p)
+            if p + AHEAD < pieces:
+                send_piece(p + AHEAD)
+                send_halo(0, p + AHEAD)
         if p > 0:
-            for k in range(nz):
-                strain_piece(k, p - 1)
-
-    index = 0
-    for i in range(frames // BLOCK):
-        width = (i + 1) * BLOCK
-        value = jnp.zeros((BLOCK, width), jnp.float32)
-        for c in range(3):
-            value += lax.dot_general(s_ref[c, i * BLOCK:(i + 1) * BLOCK, :], s_ref[c, :width, :], NT,
-                                     preferred_element_type=jnp.float32)
-        for j in range(i + 1):
-            acc[index * BLOCK:(index + 1) * BLOCK, :] = value[:, j * BLOCK:(j + 1) * BLOCK]
-            index += 1
+            strain_piece(p - 1)
+
+    packed = [(i, j) for i in range(frames // BLOCK) for j in range(i + 1)]
+    half = len(packed) // 2
+
+    def products(which):
+        mine = packed[which * half:(which + 1) * half]
+        for j0 in range(0, frames // BLOCK, 2):
+            inside = [(i, j) for i, j in mine if j0 <= j < j0 + 2]
+            if not inside:
+                continue
+            i0, i1 = min(inside)[0], max(inside)[0] + 1
+            value = jnp.zeros(((i1 - i0) * BLOCK, 2 * BLOCK), jnp.float32)
+            for c in range(3):
+                value += lax.dot_general(s_ref[c, i0 * BLOCK:i1 * BLOCK, :],
+                                         s_ref[c, j0 * BLOCK:(j0 + 2) * BLOCK, :], NT,
+                                         preferred_element_type=jnp.float32)
+            for i, j in inside:
+                index = packed.index((i, j))
+                acc[index * BLOCK:(index + 1) * BLOCK, :] = value[
+                    (i - i0) * BLOCK:(i - i0 + 1) * BLOCK, (j - j0) * BLOCK:(j - j0 + 1) * BLOCK]
+
+    def on_core(which, half_index):
+        @pl.when(core == which)
+        def _():
+            products(half_index)
+
+    on_core(0, 1)
+    on_core(1, 0)
 
     lo, place, slot, trail = 0, 0, 0, []
     for name, peers, size, split in stages:
@@ -218,6 +241,9 @@
             copy.start()
             copies.append(copy)
             slot += 1
+        if name == "core":
+            on_core(0, 0)
+            on_core(1, 1)
         keep = lo + me * size if split else lo
         at = pl.ds(pl.multiple_of(keep, 8), size)
         landing[mine, :] = acc[at, :]
@@ -251,7 +277,7 @@
     for k in range(1, nz):
         edges[k].wait_send()
     for k in range(nz):
-        for p in range(PIECES):
+        for p in range(pieces):
             up, dn, _ = halos[k, p]
             if k > 0:
                 blocks[k, p].wait_send()
@@ -268,7 +294,7 @@
 def exchange(x, nz, nt):
     fb, width = x.shape[1], x.shape[2]
     wb, frames = width // nz, fb * nz
-    nb = frames // BLOCK
+    nb, pieces = frames // BLOCK, fb // PIECE
     rows = nb * (nb + 1) // 2 * BLOCK
     stages = sum_stages(nz, nt, rows)
     landing = sum(stage[1] * stage[2] for stage in stages)
@@ -291,8 +317,8 @@
             pltpu.VMEM((rows, BLOCK), jnp.float32),
             pltpu.VMEM((landing, BLOCK), jnp.float32),
             pltpu.VMEM((rows, BLOCK), jnp.float32),
-            dma, dma((nz, PIECES)), dma((nz, PIECES)), dma((nz,)), dma((nz,)),
-            dma((nz, PIECES)), dma((nz, PIECES)), dma((nz, PIECES)), dma((nz, PIECES)),
+            dma, dma((nz, pieces)), dma((nz, pieces)), dma((nz,)), dma((nz,)),
+            dma((nz, pieces)), dma((nz, pieces)), dma((nz, pieces)), dma((nz, pieces)),
             dma((steps,)), dma((steps,)),
         ],
         compiler_params=pltpu.CompilerParams(

time: 117 us -> 117 us (level)
  no operation moved by 1% of the time
where the time goes in v3:
time: 117 us
  Pallas kernels  113 us (97%)
  local copies, waits for them, and re-layouts  2.92 us (2%)
    pallas_call x1, Pallas kernels, exchange(): pl.pallas_call(functools.partial(exchange_kernel, nz, nt, stages), out_sh...  85.6 us
    pallas_call x1, Pallas kernels, orthonormal(): pl.pallas_call(functools.partial(basis_kernel, scale), out_shape=(jax.Sha...  27.7 us
    unnamed x1, local copies, waits for them, and re-layouts  2.92 us

profile of v3, /device:TPU:0, one launch (start us, length us, event | category | flops | bytes accessed | tf_op | source)
XLA Modules:
  0.0 116.9 jit_solution(1200704575807348486)
XLA Ops:
  0.6 2.9 %copy.6 = bf16[128,2,1,4096]{3,0,1,2:T(8,128)(2,1)S(1)} copy(bf16[128,2,1,4096]{3,1,2,0:T(2,128)(2,1)} %param.1) | data formatting | bytes 4194304 | tf_op args[0]
  3.5 85.6 %shard_map.30 = (f32[1280,128]{1,0:T(8,128)S(1)}, bf16[3,512,1024]{2,1,0:T(8,128)(2,1)S(1)}) custom-call(bf16[2,128,4096]{2,1,0:T(8,128)(2,1)S(1)} %bitcast.10), custom_call_target="tpu_custom_call" | custom-call | tf_op jit(solution)/shard_map/pallas_call | solution.py:304
  89.2 27.7 %shard_map.31 = (bf16[3,512,1024]{2,1,0:T(8,128)(2,1)}, f32[512,512]{1,0:T(8,128)}) custom-call(f32[1280,128]{1,0:T(8,128)S(1)} %get-tuple-element.6.g_ref, bf16[3,512,1024]{2,1,0:T(8,128)(2,1)S(1)} %get-tuple-element.7.s_ref), custom_call_target="tpu_custom_call" | custom-call | tf_op jit(solution)/shard_map/pallas_call | solution.py:434

commit v4 on v3

--- a/solution.py
+++ b/solution.py
@@ -29,7 +29,8 @@
 
 def exchange_kernel(nz, nt, stages, x_ref, gram_ref, s_ref, center, above, below, edge_out, edge_in,
                     edge_cols, acc, landing, total, own_sem, a2a_send, a2a_recv, edge_send, edge_recv,
-                    up_send, up_recv, dn_send, dn_recv, sum_send, sum_recv):
+                    up_send, up_recv, dn_send, dn_recv, sum_send, sum_recv,
+                    relay, x_send, x_recv, v_send, v_recv, f_send, f_recv):
     z, t = lax.axis_index("frame"), lax.axis_index("tile")
     fb, wb = x_ref.shape[1], x_ref.shape[2] // nz
     frames, part, pieces = fb * nz, PIECE, fb // PIECE
@@ -45,13 +46,10 @@
 
     barrier = pltpu.get_barrier_semaphore()
     greeted = 0
-    for name, peers in (("core", 2), ("chip", chips), ("frame", nz)):
+    for name, me, peers in (("tile", t, nt), ("frame", z, nz)):
         for k in range(1, peers):
-            pl.semaphore_signal(barrier, inc=1, device_id=member(name, k)[2], device_id_type=MESH)
+            pl.semaphore_signal(barrier, inc=1, device_id={name: lax.rem(me + k, peers)}, device_id_type=MESH)
             greeted += 1
-    for k in (1, nt - 1):
-        pl.semaphore_signal(barrier, inc=1, device_id={"tile": lax.rem(t + k, nt)}, device_id_type=MESH)
-        greeted += 1
     pl.semaphore_wait(barrier, greeted)
 
     def frame_rows(s, p):
@@ -74,7 +72,14 @@
             copy.start()
             blocks[k, p] = copy
 
-    halos = {}
+    halos, corners = {}, {}
+    corner = nt == 8
+    low, high = nt // 2 - 1, nt // 2
+    sends_up, sends_dn = t < nt - 1, t > 0
+    gets_above, gets_below = t > 0, t < nt - 1
+    if corner:
+        sends_up, sends_dn = sends_up & (t != low), sends_dn & (t != high)
+        gets_above, gets_below = gets_above & (t != high), gets_below & (t != low)
 
     def send_halo(k, p):
         s = lax.rem(z - k + nz, nz)
@@ -90,13 +95,57 @@
             device_id={"tile": lax.rem(t + nt - 1, nt)}, device_id_type=MESH)
         halos[k, p] = (up, dn, s)
 
-        @pl.when(t < nt - 1)
+        @pl.when(sends_up)
         def _():
             up.start()
 
-        @pl.when(t > 0)
+        @pl.when(sends_dn)
         def _():
             dn.start()
+
+        if not corner:
+            return
+
+        def cross(target):
+            return pltpu.make_async_remote_copy(
+                src_ref=src.at[0], dst_ref=target.at[0, rows, :],
+                send_sem=x_send.at[k, p], recv_sem=x_recv.at[k, p],
+                device_id={"tile": nt - 1 - t}, device_id_type=MESH)
+
+        def onward(target):
+            return pltpu.make_async_remote_copy(
+                src_ref=relay.at[rows, :], dst_ref=target.at[1, rows, :],
+                send_sem=f_send.at[k, p], recv_sem=f_recv.at[k, p],
+                device_id={"tile": low + t // (nt - 1)}, device_id_type=MESH)
+
+        via = pltpu.make_async_remote_copy(
+            src_ref=src.at[1], dst_ref=relay.at[rows, :],
+            send_sem=v_send.at[k, p], recv_sem=v_recv.at[k, p],
+            device_id={"tile": (nt - 1) * (high - t)}, device_id_type=MESH)
+        corners[k, p] = (cross(above), cross(below), via, onward(above), onward(below))
+
+        @pl.when(t == low)
+        def _():
+            via.start()
+            corners[k, p][0].start()
+
+        @pl.when(t == high)
+        def _():
+            via.start()
+            corners[k, p][1].start()
+
+    def forward(k, p):
+        _, _, via, on_above, on_below = corners[k, p]
+
+        @pl.when(t == nt - 1)
+        def _():
+            via.wait_recv()
+            on_above.start()
+
+        @pl.when(t == 0)
+        def _():
+            via.wait_recv()
+            on_below.start()
 
     row16 = lax.broadcasted_iota(jnp.int32, (16, 128), 0)
     lane16 = lax.broadcasted_iota(jnp.int32, (16, 128), 1)
@@ -129,9 +178,10 @@
 
     for p in range(min(AHEAD, pieces)):
         send_piece(p)
-        send_halo(0, p)
         if p == 0:
             send_edges()
+    for p in range(pieces):
+        send_halo(0, p)
 
     own.wait()
 
@@ -146,13 +196,26 @@
         for k in range(nz):
             up, dn, s = halos[k, p]
 
-            @pl.when(t > 0)
+            @pl.when(gets_above)
             def _(up=up):
                 up.wait_recv()
 
-            @pl.when(t < nt - 1)
+            @pl.when(gets_below)
             def _(dn=dn):
                 dn.wait_recv()
+
+            if corner:
+                over, under, _, on_above, on_below = corners[k, p]
+
+                @pl.when(t == high)
+                def _(over=over, on_above=on_above):
+                    over.wait_recv()
+                    on_above.wait_recv()
+
+                @pl.when(t == low)
+                def _(under=under, on_below=on_below):
+                    under.wait_recv()
+                    on_below.wait_recv()
 
             if p == 0:
                 if k > 0:
@@ -194,8 +257,10 @@
                 send_halo(k, p)
             if p + AHEAD < pieces:
                 send_piece(p + AHEAD)
-                send_halo(0, p + AHEAD)
         if p > 0:
+            if corner:
+                for k in range(nz):
+                    forward(k, p - 1)
             strain_piece(p - 1)
 
     packed = [(i, j) for i in range(frames // BLOCK) for j in range(i + 1)]
@@ -282,13 +347,34 @@
             if k > 0:
                 blocks[k, p].wait_send()
 
-            @pl.when(t < nt - 1)
+            @pl.when(sends_up)
             def _(up=up):
                 up.wait_send()
 
-            @pl.when(t > 0)
+            @pl.when(sends_dn)
             def _(dn=dn):
                 dn.wait_send()
+
+            if corner:
+                over, under, via, on_above, on_below = corners[k, p]
+
+                @pl.when(t == low)
+                def _(over=over, via=via):
+                    over.wait_send()
+                    via.wait_send()
+
+                @pl.when(t == high)
+                def _(under=under, via=via):
+                    under.wait_send()
+                    via.wait_send()
+
+                @pl.when(t == nt - 1)
+                def _(on_above=on_above):
+                    on_above.wait_send()
+
+                @pl.when(t == 0)
+                def _(on_below=on_below):
+                    on_below.wait_send()
 
 
 def exchange(x, nz, nt):
@@ -320,6 +406,9 @@
             dma, dma((nz, pieces)), dma((nz, pieces)), dma((nz,)), dma((nz,)),
             dma((nz, pieces)), dma((nz, pieces)), dma((nz, pieces)), dma((nz, pieces)),
             dma((steps,)), dma((steps,)),
+            pltpu.VMEM((frames, wb), jnp.bfloat16),
+            dma((nz, pieces)), dma((nz, pieces)), dma((nz, pieces)),
+            dma((nz, pieces)), dma((nz, pieces)), dma((nz, pieces)),
         ],
         compiler_params=pltpu.CompilerParams(
             collective_id=0, has_side_effects=True, vmem_limit_bytes=40 * 1024 * 1024),

time: 117 us -> 118 us (level)
  Pallas kernels: 113 us -> 115 us
    pallas_call x1, Pallas kernels: 85.6 us -> 86.9 us  [exchange(): pl.pallas_call(functools.partial(exchange_kernel, nz, nt, stages), out_sh...]
where the time goes in v4:
time: 118 us
  Pallas kernels  115 us (97%)
  local copies, waits for them, and re-layouts  2.92 us (2%)
    pallas_call x1, Pallas kernels, exchange(): pl.pallas_call(functools.partial(exchange_kernel, nz, nt, stages), out_sh...  86.9 us
    pallas_call x1, Pallas kernels, orthonormal(): pl.pallas_call(functools.partial(basis_kernel, scale), out_shape=(jax.Sha...  27.7 us
    unnamed x1, local copies, waits for them, and re-layouts  2.92 us

profile of v4, /device:TPU:0, one launch (start us, length us, event | category | flops | bytes accessed | tf_op | source)
XLA Modules:
  0.0 118.2 jit_solution(1210370937354292910)
XLA Ops:
  0.6 2.9 %copy.6 = bf16[128,2,1,4096]{3,0,1,2:T(8,128)(2,1)S(1)} copy(bf16[128,2,1,4096]{3,1,2,0:T(2,128)(2,1)} %param.1) | data formatting | bytes 4194304 | tf_op args[0]
  3.5 86.9 %shard_map.30 = (f32[1280,128]{1,0:T(8,128)S(1)}, bf16[3,512,1024]{2,1,0:T(8,128)(2,1)S(1)}) custom-call(bf16[2,128,4096]{2,1,0:T(8,128)(2,1)S(1)} %bitcast.10), custom_call_target="tpu_custom_call" | custom-call | tf_op jit(solution)/shard_map/pallas_call | solution.py:390
  90.5 27.7 %shard_map.31 = (bf16[3,512,1024]{2,1,0:T(8,128)(2,1)}, f32[512,512]{1,0:T(8,128)}) custom-call(f32[1280,128]{1,0:T(8,128)S(1)} %get-tuple-element.6.g_ref, bf16[3,512,1024]{2,1,0:T(8,128)(2,1)S(1)} %get-tuple-element.7.s_ref), custom_call_target="tpu_custom_call" | custom-call | tf_op jit(solution)/shard_map/pallas_call | solution.py:523

commit v5 on v3

--- a/solution.py
+++ b/solution.py
@@ -27,7 +27,7 @@
     return stages
 
 
-def exchange_kernel(nz, nt, stages, x_ref, gram_ref, s_ref, center, above, below, edge_out, edge_in,
+def exchange_kernel(nz, nt, stages, raw_ref, gram_ref, s_ref, x_ref, center, above, below, edge_out, edge_in,
                     edge_cols, acc, landing, total, own_sem, a2a_send, a2a_recv, edge_send, edge_recv,
                     up_send, up_recv, dn_send, dn_recv, sum_send, sum_recv):
     z, t = lax.axis_index("frame"), lax.axis_index("tile")
@@ -42,6 +42,10 @@
         if name == "chip":
             return chip, lax.rem(chip + k, chips), {"tile": lax.rem(chip + k, chips) * 2 + core}
         return z, lax.rem(z + k, nz), {"frame": lax.rem(z + k, nz)}
+
+    def separate(p):
+        for c in range(2):
+            x_ref[c, p * part:(p + 1) * part, :] = raw_ref[p * part:(p + 1) * part, c, :]
 
     barrier = pltpu.get_barrier_semaphore()
     greeted = 0
@@ -52,15 +56,14 @@
     for k in (1, nt - 1):
         pl.semaphore_signal(barrier, inc=1, device_id={"tile": lax.rem(t + k, nt)}, device_id_type=MESH)
         greeted += 1
+    for p in range(min(AHEAD, pieces)):
+        separate(p)
     pl.semaphore_wait(barrier, greeted)
 
     def frame_rows(s, p):
         return pl.ds(pl.multiple_of(s * fb + p * part, 16), part)
 
     own_cols = pl.ds(pl.multiple_of(z * wb, 128), wb)
-    own = pltpu.make_async_copy(
-        x_ref.at[:, :, own_cols], center.at[:, pl.ds(pl.multiple_of(z * fb, 16), fb), :], own_sem)
-    own.start()
     blocks = {}
 
     def send_piece(p):
@@ -130,9 +133,13 @@
     for p in range(min(AHEAD, pieces)):
         send_piece(p)
         send_halo(0, p)
-        if p == 0:
-            send_edges()
-
+    for p in range(AHEAD, pieces):
+        separate(p)
+    send_edges()
+
+    own = pltpu.make_async_copy(
+        x_ref.at[:, :, own_cols], center.at[:, pl.ds(pl.multiple_of(z * fb, 16), fb), :], own_sem)
+    own.start()
     own.wait()
 
     lane = lax.broadcasted_iota(jnp.int32, (16, wb), 1)
@@ -292,7 +299,7 @@
 
 
 def exchange(x, nz, nt):
-    fb, width = x.shape[1], x.shape[2]
+    fb, width = x.shape[0], x.shape[2]
     wb, frames = width // nz, fb * nz
     nb, pieces = frames // BLOCK, fb // PIECE
     rows = nb * (nb + 1) // 2 * BLOCK
@@ -308,6 +315,7 @@
         in_specs=[vmem],
         out_specs=(vmem, vmem),
         scratch_shapes=[
+            pltpu.VMEM((2, fb, width), jnp.bfloat16),
             pltpu.VMEM((2, frames, wb), jnp.bfloat16),
             pltpu.VMEM((2, frames, wb), jnp.bfloat16),
             pltpu.VMEM((2, frames, wb), jnp.bfloat16),
@@ -377,7 +385,7 @@
     return jnp.concatenate(left, axis=0), jnp.concatenate(right, axis=0)
 
 
-def basis_kernel(scale, g_ref, s_ref, basis_ref, factor_ref, work, planes):
+def basis_kernel(scale, g_ref, s_ref, basis_ref, factor_ref, work, planes, staged, out_sem):
     n = factor_ref.shape[0]
     wide = n // 2
     nb = n // BLOCK
@@ -424,7 +432,10 @@
         for i in range(n // wide):
             depth = (i + 1) * wide
             value = jnp.dot(planes[i, :, :depth], s_ref[c, :depth, :], preferred_element_type=jnp.float32)
-            basis_ref[c, i * wide:(i + 1) * wide, :] = (value[:wide] + value[wide:]).astype(jnp.bfloat16)
+            staged[c, i * wide:(i + 1) * wide, :] = (value[:wide] + value[wide:]).astype(jnp.bfloat16)
+        pltpu.make_async_copy(staged.at[c], basis_ref.at[c], out_sem.at[c]).start()
+    for c in range(3):
+        pltpu.make_async_copy(staged.at[c], basis_ref.at[c], out_sem.at[c]).wait()
 
 
 def orthonormal(gram, strain, scale):
@@ -436,10 +447,12 @@
         out_shape=(jax.ShapeDtypeStruct(strain.shape, jnp.bfloat16),
                    jax.ShapeDtypeStruct((frames, frames), jnp.float32)),
         in_specs=[vmem, vmem],
-        out_specs=(vmem, vmem),
+        out_specs=(pl.BlockSpec(memory_space=pl.ANY), vmem),
         scratch_shapes=[
             pltpu.VMEM((nb, BLOCK, 2 * frames), jnp.float32),
             pltpu.VMEM((2, frames, frames), jnp.bfloat16),
+            pltpu.VMEM(strain.shape, jnp.bfloat16),
+            pltpu.SemaphoreType.DMA((3,)),
         ],
         compiler_params=pltpu.CompilerParams(vmem_limit_bytes=40 * 1024 * 1024),
     )(gram, strain)
@@ -448,7 +461,7 @@
 def local(nz, nt, displacement):
     frames, rows, width = displacement.shape[0] * nz, displacement.shape[2] * nt, displacement.shape[3]
     scale = math.sqrt(3 * rows * width)
-    x = jnp.transpose(displacement[:, :, 0, :], (1, 0, 2))
+    x = displacement[:, :, 0, :]
     gram, strain = exchange(x, nz, nt)
     basis, factor = orthonormal(gram, strain, scale)
     return jnp.transpose(basis, (1, 0, 2))[:, :, None, :], factor

time: 117 us -> 115 us (0.983)
  local copies, waits for them, and re-layouts: 2.92 us -> 1.58 us
    unnamed x1 -> x2, local copies, waits for them, and re-layouts: 2.92 us -> 1.58 us
where the time goes in v5:
time: 115 us
  Pallas kernels  113 us (98%)
  local copies, waits for them, and re-layouts  1.58 us (1%)
    pallas_call x1, Pallas kernels, exchange(): pl.pallas_call(functools.partial(exchange_kernel, nz, nt, stages), out_sh...  84.9 us
    pallas_call x1, Pallas kernels, orthonormal(): pl.pallas_call(functools.partial(basis_kernel, scale), out_shape=(jax.Sha...  27.8 us

profile of v5, /device:TPU:0, one launch (start us, length us, event | category | flops | bytes accessed | tf_op | source)
XLA Modules:
  0.0 115.1 jit_solution(10520986235879550164)
XLA Ops:
  0.6 0.0 copy-start
  0.6 1.6 %copy-done = bf16[128,2,1,4096]{3,1,2,0:T(2,128)(2,1)S(1)} copy-done((bf16[128,2,1,4096]{3,1,2,0:T(2,128)(2,1)S(1)}, bf16[128,2,1,4096]{3,1,2,0:T(2,128)(2,1)}, u32[]{:S(2)}) %copy-start) | copy-done | bytes 2097176
  2.2 84.9 %shard_map.30 = (f32[1280,128]{1,0:T(8,128)S(1)}, bf16[3,512,1024]{2,1,0:T(8,128)(2,1)S(1)}) custom-call(bf16[128,2,4096]{2,1,0:T(2,128)(2,1)S(1)} %bitcast.6), custom_call_target="tpu_custom_call" | custom-call | tf_op jit(solution)/shard_map/pallas_call | solution.py:311
  87.2 27.8 %shard_map.31 = (bf16[3,512,1024]{2,1,0:T(8,128)(2,1)}, f32[512,512]{1,0:T(8,128)}) custom-call(f32[1280,128]{1,0:T(8,128)S(1)} %get-tuple-element.6.g_ref, bf16[3,512,1024]{2,1,0:T(8,128)(2,1)S(1)} %get-tuple-element.7.s_ref), custom_call_target="tpu_custom_call" | custom-call | tf_op jit(solution)/shard_map/pallas_call | solution.py:445
Async XLA Ops:
  0.6 1.6 %copy-start = (bf16[128,2,1,4096]{3,1,2,0:T(2,128)(2,1)S(1)}, bf16[128,2,1,4096]{3,1,2,0:T(2,128)(2,1)}, u32[]{:S(2)}) copy-start(bf16[128,2,1,4096]{3,1,2,0:T(2,128)(2,1)} %param.1) | copy-start | bytes 6291460
